TPU v7x, 512 devices: a whole 4x8x8 slice. The times are simulated.
512 devices in a mesh: loop: 16 (over x, z_lo), bulk: 32 (over z_hi, y, core).
Axes of the slice: x: 4, y: 8, z: 8 (z_hi: 2, z_lo: 4; z = z_hi * 4 + z_lo), core: 2. Of those that a mesh axis runs over, the one named last changes fastest.
Arguments:
- series: float32 [16896, 3072], P('loop', 'bulk'), may hold values from -64 to 64
Outputs:
- correlation: float32 [16, 1056, 16896], P(None, 'bulk', 'loop')
All inputs are finite; a program needn't handle non-finite values.
Results may differ from a plain program's by a relative error of at most 0.0011.
Values may be sent and summed in bfloat16 or wider, within the bound.
No kernel may reach another device: no remote copies, remote signals or barrier semaphores. Data moves between devices by JAX's collectives and lax.ppermute only.
A program may use at most 64 MiB of HBM per device.

v0:
```python
import jax
import jax.numpy as jnp
from jax import lax
from jax.sharding import PartitionSpec as P

TIME = 3072
epsilon = 1e-06


def standardize(rows):
    average = jnp.sum(rows, axis=1, keepdims=True) / TIME
    centered = rows - average
    variance = jnp.sum(centered * centered, axis=1, keepdims=True) / TIME
    return (centered * lax.rsqrt(variance + epsilon)).astype(jnp.bfloat16)


def on_device(series):
    n_bulk = lax.axis_size("bulk")
    rows, steps = series.shape
    share = rows // n_bulk
    pieces = lax.all_to_all(series.reshape(n_bulk, share, steps), "bulk", 0, 0, tiled=True)
    own = standardize(pieces.transpose(1, 0, 2).reshape(share, n_bulk * steps))
    block = lax.all_gather(own, "bulk", axis=0, tiled=True)
    others = lax.all_gather(own, "loop", axis=0, tiled=True)
    product = lax.dot_general(
        others, block, (((1,), (1,)), ((), ())), preferred_element_type=jnp.float32
    )
    return (product / TIME).reshape(lax.axis_size("loop"), share, rows)


def solution(mesh):
    placed = (P("loop", "bulk"),)
    return jax.shard_map(
        on_device, mesh=mesh, in_specs=placed, out_specs=P(None, "bulk", "loop"), check_vma=False
    )
```

profile of v0, /device:TPU:1, one launch (start us, length us, event | category | flops | bytes accessed | tf_op | source)
XLA Modules:
  0.0 305.6 jit_solution(10203501590802974913)
XLA Ops:
  6.5 0.0 all-gather.5.cloned.1.call-start
  6.5 1.2 copy.6
  7.8 39.9 %all_to_all.5 = f32[32,33,96]{2,1,0:T(8,128)S(1)} all-to-all(f32[32,33,96]{2,1,0:T(8,128)S(1)} %reshape.26), channel_id=1, replica_groups=mesh['loop'=16,'bulk'=32] {'bulk'}, dimensions={0} | all-to-all | bytes 811008 | tf_op jit(solution)/shard_map/all_to_all | solution.py:21
  47.7 0.2 reduce_sum.18
  47.9 0.3 multiply_reduce_fusion
  48.2 0.1 copy.7
  48.3 0.3 reshape.27
  48.6 0.8 fusion
  49.4 0.0 all-gather.5.cloned.1.call-update
  49.4 0.0 all-gather.7.cloned.1.call-start
  49.5 0.7 all-gather.7.cloned.1.call-update
  50.2 91.8 %all-gather.5.cloned.1.call-done = bf16[16,33,3072]{2,1,0:T(8,128)(2,1)} async-done(((bf16[1,33,3072]{2,1,0:T(8,128)(2,1)}), bf16[16,33,3072]{2,1,0:T(8,128)(2,1)}) %all-gather.5.cloned.1.call-update) | async-done | bytes 3244048 | tf_op jit(solution)/shard_map/all_gather | solution.py:24
  142.0 2.7 reshape.30
  144.7 134.6 %all-gather.7.cloned.1.call-done = bf16[32,33,3072]{2,1,0:T(8,128)(2,1)} async-done(((bf16[1,33,3072]{2,1,0:T(8,128)(2,1)}), bf16[32,33,3072]{2,1,0:T(8,128)(2,1)}) %all-gather.7.cloned.1.call-update) | async-done | bytes 6488080 | tf_op jit(solution)/shard_map/all_gather | solution.py:23
  279.3 7.1 %reshape.32 = bf16[1056,3072]{1,0:T(8,128)(2,1)} reshape(bf16[32,33,3072]{2,1,0:T(8,128)(2,1)} %all-gather.7.cloned.1.call-done) | data formatting | bytes 12976128
  286.4 8.7 %convolution_multiply_fusion = f32[528,1056]{1,0:T(8,128)} fusion(bf16[528,3072]{1,0:T(8,128)(2,1)S(1)} %reshape.30, bf16[1056,3072]{1,0:T(8,128)(2,1)} %reshape.32), kind=kOutput, calls=%fused_computation | convolution fusion | flops 3426255360 | bytes 11962368 | tf_op jit(solution)/shard_map/dot_general | solution.py:25
  295.1 1.8 reshape.28
  296.9 1.9 copy.8
  (3 shorter events, 0.1 us)
Async XLA Ops:
  6.5 135.5 %all-gather.5.cloned.1.call-start = ((), (), s32[]{:S(2)}) async-start(), calls=%async_computation.1 | async-start | bytes 4177920 | tf_op jit(solution)/shard_map/all_gather | solution.py:24
  49.4 229.9 %all-gather.7.cloned.1.call-start = ((), (), s32[]{:S(2)}) async-start(), calls=%async_computation.2 | async-start | bytes 8110080 | tf_op jit(solution)/shard_map/all_gather | solution.py:23
Sparse Core Ops, SparseCore 0:
  49.5 92.4 all-gather.4
  145.4 133.8 all-gather.6
where the time goes:
time: 306 us
  waiting for transfers between devices  227 us (74%)
  blocking collectives  39.9 us (13%)
  local copies, waits for them, and re-layouts  15.2 us (5%)
  between operations  13.4 us (4%)
  matrix products  8.65 us (3%)
    all_gather x1, waiting for transfers between devices, on_device(): block = lax.all_gather(own, 'bulk', axis=0, tiled=True)  135 us
    all_gather x1, waiting for transfers between devices, on_device(): others = lax.all_gather(own, 'loop', axis=0, tiled=True)  91.8 us
    all_to_all x1, blocking collectives, on_device(): lax.all_to_all(series.reshape(n_bulk, share, steps), 'bulk', 0, 0, tiled=...  39.9 us
    unnamed x3, local copies, waits for them, and re-layouts  11 us
    dot_general x1, matrix products, on_device(): lax.dot_general(others, block, (((1,), (1,)), ((), ())), preferred_elemen...  8.65 us
  transfers between devices with their start and end apart: 2, of which 2 were waited for; matrix products, arithmetic and copies ran while one was open for 1% of the time, Pallas kernels for 0%

commit v1 on v0

--- a/solution.py
+++ b/solution.py
@@ -5,6 +5,13 @@
 
 TIME = 3072
 epsilon = 1e-06
+
+
+def exchange_gather(x, axis, dim):
+    devices = lax.axis_size(axis)
+    tiles = jnp.stack([x for _ in range(devices)])
+    tiles = lax.all_to_all(tiles, axis, split_axis=0, concat_axis=0)
+    return jnp.concatenate(tiles, axis=dim)
 
 
 def standardize(rows):
@@ -21,7 +28,7 @@
     pieces = lax.all_to_all(series.reshape(n_bulk, share, steps), "bulk", 0, 0, tiled=True)
     own = standardize(pieces.transpose(1, 0, 2).reshape(share, n_bulk * steps))
     block = lax.all_gather(own, "bulk", axis=0, tiled=True)
-    others = lax.all_gather(own, "loop", axis=0, tiled=True)
+    others = exchange_gather(own, "loop", 0)
     product = lax.dot_general(
         others, block, (((1,), (1,)), ((), ())), preferred_element_type=jnp.float32
     )

time: 306 us -> 223 us (0.73)
  waiting for transfers between devices: 227 us -> 0.04 us
  blocking collectives: 39.9 us -> 183 us
    all_to_all x0 -> x1, blocking collectives: none -> 143 us  [exchange_gather(): tiles = lax.all_to_all(tiles, axis, split_axis=0, concat_axis=0)]
    all_gather x1, waiting for transfers between devices: 135 us -> 0.02 us  [on_device(): block = lax.all_gather(own, 'bulk', axis=0, tiled=True)]
    all_gather x1 -> x0, waiting for transfers between devices: 91.8 us -> none  [on_device(): others = lax.all_gather(own, 'loop', axis=0, tiled=True)]
    unnamed x3 -> x2, local copies, waits for them, and re-layouts: 11 us -> 8.34 us
  transfers between devices with their start and end apart: 2 -> 1, of which waited for: 2 -> 0; matrix products, arithmetic and copies ran while one was open for 1% -> 1% of each run, Pallas kernels for 0% -> 0%
where the time goes in v1:
time: 223 us; the launch traced here: 222 us
  blocking collectives  183 us (82%)
  local copies, waits for them, and re-layouts  15.7 us (7%)
  between operations  13.5 us (6%)
  matrix products  8.65 us (4%)
    all_to_all x1, blocking collectives, exchange_gather(): tiles = lax.all_to_all(tiles, axis, split_axis=0, concat_axis=0)  143 us
    all_to_all x1, blocking collectives, on_device(): lax.all_to_all(series.reshape(n_bulk, share, steps), 'bulk', 0, 0, tiled=...  39.9 us
    dot_general x1, matrix products, on_device(): lax.dot_general(others, block, (((1,), (1,)), ((), ())), preferred_elemen...  8.65 us
    unnamed x2, local copies, waits for them, and re-layouts  8.34 us
  transfers between devices with their start and end apart: 1, of which 0 were waited for; matrix products, arithmetic and copies ran while one was open for 1% of the time, Pallas kernels for 0%

profile of v1, /device:TPU:1, one launch (start us, length us, event | category | flops | bytes accessed | tf_op | source)
XLA Modules:
  0.0 222.0 jit_solution(14022128890702746791)
XLA Ops:
  6.5 0.0 all-gather.3.cloned.1.call-start
  6.5 1.2 copy.6
  7.8 39.9 %all_to_all.10 = f32[32,33,96]{2,1,0:T(8,128)S(1)} all-to-all(f32[32,33,96]{2,1,0:T(8,128)S(1)} %reshape.44), channel_id=1, replica_groups=mesh['loop'=16,'bulk'=32] {'bulk'}, dimensions={0} | all-to-all | bytes 811008 | tf_op jit(solution)/shard_map/all_to_all | solution.py:28
  47.7 0.2 reduce_sum.18
  47.9 0.3 multiply_reduce_fusion
  48.2 0.1 copy.7
  48.3 0.3 reshape.45
  48.6 0.8 fusion.2
  49.4 0.0 all-gather.3.cloned.1.call-update
  49.4 0.1 multiply_convert_fusion
  49.5 0.5 stack.2
  50.0 142.9 %all_to_all.11 = bf16[16,33,3072]{2,1,0:T(8,128)(2,1)} all-to-all(bf16[16,33,3072]{2,1,0:T(8,128)(2,1)S(1)} %stack.2), channel_id=1, replica_groups=mesh['loop'=16,'bulk'=32] {'loop'}, dimensions={0} | all-to-all | bytes 6488064 | tf_op jit(solution)/shard_map/all_to_all | solution.py:13
  192.9 2.7 %reshape.46 = bf16[528,3072]{1,0:T(8,128)(2,1)S(1)} reshape(bf16[16,33,3072]{2,1,0:T(8,128)(2,1)} %all_to_all.11) | data formatting | bytes 6488064 | tf_op jit(solution)/shard_map/reshape | solution.py:14
  195.6 0.0 all-gather.3.cloned.1.call-done
  195.6 7.1 %reshape.49 = bf16[1056,3072]{1,0:T(8,128)(2,1)} reshape(bf16[32,33,3072]{2,1,0:T(8,128)(2,1)} %all-gather.3.cloned.1.call-done) | data formatting | bytes 12976128
  202.8 8.7 %convolution_multiply_fusion = f32[528,1056]{1,0:T(8,128)} fusion(bf16[528,3072]{1,0:T(8,128)(2,1)S(1)} %reshape.46, bf16[1056,3072]{1,0:T(8,128)(2,1)} %reshape.49), kind=kOutput, calls=%fused_computation | convolution fusion | flops 3426255360 | bytes 11962368 | tf_op jit(solution)/shard_map/dot_general | solution.py:32
  211.4 1.8 reshape.47
  213.2 1.9 copy.8
  (3 shorter events, 0.1 us)
Async XLA Ops:
  6.5 189.1 %all-gather.3.cloned.1.call-start = ((), (), s32[]{:S(2)}) async-start(), calls=%async_computation.2 | async-start | bytes 8110080 | tf_op jit(solution)/shard_map/all_gather | solution.py:30
Sparse Core Ops, SparseCore 0:
  49.5 143.5 all-gather.2
